TPU v7x, 256 devices: a whole 4x4x8 slice. The times are simulated.
256 devices in a mesh: seq: 64 (over y_lo, x, z), batch: 4 (over y_hi, core).
Axes of the slice: x: 4, y: 4 (y_hi: 2, y_lo: 2; y = y_hi * 2 + y_lo), z: 8, core: 2. Of those that a mesh axis runs over, the one named last changes fastest.
Arguments:
- queries: bfloat16 [512, 1024], replicated, may hold values from -48 to 48
- inputs: bfloat16 [4, 49152, 1024], P('batch', 'seq'), may hold values from -18 to 18
- cotangent: bfloat16 [4, 512, 1024], P('batch'), may hold values from -48 to 48
- key_weight: bfloat16 [1024, 1024], replicated, may hold values from -0.1875 to 0.1875
- value_weight: bfloat16 [1024, 1024], replicated, may hold values from -0.1875 to 0.1875
Outputs:
- input_grad: bfloat16 [4, 49152, 1024], P('batch', 'seq')
- latent_grad: float32 [512, 1024], P('seq')
- key_weight_grad: float32 [1024, 1024], P('seq')
- value_weight_grad: float32 [1024, 1024], P('seq')
All inputs are finite; a program needn't handle non-finite values.
Results may differ from a plain program's by a relative error of at most 0.015.
The roundings to bfloat16 on the way count: a program that leaves them out, or rounds other values in their place, can miss the bound.
Values sent between devices are 32-bit elements; how exact they have to be, the bound alone decides.
No kernel may reach another device: no remote copies, remote signals or barrier semaphores. Data moves between devices by JAX's collectives and lax.ppermute only.
A program may use at most 128 MiB of HBM per device.

v0:
```python
import jax
import jax.numpy as jnp
from jax import lax
from jax.sharding import PartitionSpec as P

H = 8


def body(queries, inputs, cotangent, key_weight, value_weight):
    features = inputs[0]
    cot_rows = cotangent[0]
    positions = features.shape[0]
    latents, width = queries.shape
    heads = H
    head_size = width // heads
    score_scale = 1.0 / jnp.sqrt(jnp.float32(head_size))
    key_proj = jnp.dot(features, key_weight, preferred_element_type=jnp.float32).astype(
        jnp.bfloat16
    )
    value_proj = jnp.dot(features, value_weight, preferred_element_type=jnp.float32).astype(
        jnp.bfloat16
    )
    queries_by_head = queries.reshape(latents, heads, head_size)
    keys_by_head = key_proj.reshape(positions, heads, head_size)
    values_by_head = value_proj.reshape(positions, heads, head_size)
    cotangent_per_head = cot_rows.reshape(latents, heads, head_size)
    scores = (
        jnp.einsum(
            "gfw,rfw->fgr", queries_by_head, keys_by_head, preferred_element_type=jnp.float32
        )
        * score_scale
    )
    probability_gradient = jnp.einsum(
        "gfw,rfw->fgr", cotangent_per_head, values_by_head, preferred_element_type=jnp.float32
    )
    local_top = jnp.max(scores, axis=-1)
    global_top = lax.pmax(local_top, "seq")
    expo = jnp.exp(scores - global_top[:, :, None])
    part_total = jnp.sum(expo, axis=-1)
    part_delta = jnp.sum(expo * probability_gradient, axis=-1)
    row_total, delta_raw = lax.psum((part_total, part_delta), "seq")
    softmax = expo / row_total[:, :, None]
    row_delta = delta_raw / row_total
    score_gradient = (softmax * (probability_gradient - row_delta[:, :, None])).astype(jnp.bfloat16)
    softmax_probabilities = softmax.astype(jnp.bfloat16)
    dquery = (
        jnp.einsum("zua,azn->uzn", score_gradient, keys_by_head, preferred_element_type=jnp.float32)
        * score_scale
    ).reshape(latents, width)
    dkeys = (
        (
            jnp.einsum(
                "iyf,yit->fit", score_gradient, queries_by_head, preferred_element_type=jnp.float32
            )
            * score_scale
        )
        .astype(jnp.bfloat16)
        .reshape(positions, width)
    )
    dvalues = (
        jnp.einsum(
            "iyf,yit->fit",
            softmax_probabilities,
            cotangent_per_head,
            preferred_element_type=jnp.float32,
        )
        .astype(jnp.bfloat16)
        .reshape(positions, width)
    )
    both_grads = jnp.concatenate([dkeys, dvalues], axis=1)
    seq_count = lax.axis_size("seq")
    weight_part = lax.psum_scatter(
        lax.dot_general(
            features, both_grads, (((0,), (0,)), ((), ())), preferred_element_type=jnp.float32
        ),
        "seq",
        scatter_dimension=0,
        tiled=True,
    )
    weight_sums = lax.psum(weight_part, "batch")
    grad_in = jnp.dot(dkeys, key_weight.T, preferred_element_type=jnp.float32) + jnp.dot(
        dvalues, value_weight.T, preferred_element_type=jnp.float32
    )
    row_share = latents // seq_count
    query_sums = lax.psum(dquery, ("seq", "batch"))
    latent_grad = lax.dynamic_slice_in_dim(
        query_sums, lax.axis_index("seq") * row_share, row_share, 0
    )
    return (
        grad_in.astype(jnp.bfloat16)[None],
        latent_grad,
        weight_sums[:, :width],
        weight_sums[:, width:],
    )


def solution(mesh):
    placed = (P(), P("batch", "seq", None), P("batch", None, None), P(), P())
    return jax.shard_map(
        body,
        mesh=mesh,
        in_specs=placed,
        out_specs=(P("batch", "seq", None), P("seq", None), P("seq", None), P("seq", None)),
        check_vma=False,
    )
```

profile of v0, /device:TPU:1, one launch (start us, length us, event | category | flops | bytes accessed | tf_op | source)
XLA Modules:
  0.0 1078.5 jit_solution(4048435747894452851)
XLA Ops:
  8.0 0.0 reduce-scatter.4.cloned.1.call-start
  8.1 1.5 copy-done
  9.6 4.3 convolution_convert_fusion.1
  13.9 2.6 copy.40
  16.5 1.5 copy.41
  18.0 7.8 bitcast_reduce_fusion
  25.8 257.1 %pmax.7 = f32[8,512]{1,0:T(8,128)S(1)} all-reduce(f32[8,512]{1,0:T(8,128)S(1)} %get-tuple-element.18), channel_id=1, replica_groups=mesh['seq'=64,'batch'=4] {'seq'}, use_global_device_ids=true, to_apply=%region_1.0 | all-reduce | flops 4096 | bytes 32768 | tf_op jit(solution)/shard_map/pmax | solution.py:37
  282.9 2.3 copy.42
  285.2 3.9 fusion.21
  289.2 8.8 fusion.5
  298.0 248.4 %all-reduce = (f32[8,512]{1,0:T(8,128)S(1)}, f32[8,512]{1,0:T(8,128)S(1)}) all-reduce(f32[8,512]{1,0:T(8,128)S(1)} %get-tuple-element.13, f32[8,512]{1,0:T(8,128)S(1)} %get-tuple-element.12), channel_id=1, replica_groups=mesh['seq'=64,'batch'=4] {'seq'}, use_global_device_ids=true, to_apply=%region_5.0 | all-reduce | flops 8192 | bytes 65536 | tf_op jit(solution)/shard_map/psum | solution.py:41
  546.4 7.7 fusion.12
  554.2 10.3 fusion.2
  564.5 2.2 multiply_convert_fusion
  566.7 0.5 copy-done.1
  567.1 1.1 copy-done.5
  568.3 7.0 convolution_bitcast_fusion
  575.3 9.1 copy.38
  584.5 0.0 all-reduce.4.cloned.1.call-start
  584.5 5.7 convolution_multiply_fusion
  590.2 3.0 copy.32
  593.2 0.0 all-reduce.4.cloned.1.call-update
  593.2 0.3 all-reduce.6.cloned.1.call-start
  593.5 5.0 fusion.28
  598.5 374.2 %reduce-scatter.4.cloned.1.call-done = f32[16,2048]{1,0:T(8,128)} async-done(((f32[1024,2048]{1,0:T(8,128)}), f32[16,2048]{1,0:T(8,128)}) %reduce-scatter.4.cloned.1.call-update) | async-done | bytes 131088
  972.6 2.2 copy.39
  974.9 6.1 fusion.24
  981.0 1.4 constant_dynamic-slice_fusion
  982.3 85.9 %all-reduce.6.cloned.1.call-done = f32[16,2048]{0,1:T(8,128)} async-done(((f32[16,2048]{0,1:T(8,128)}), f32[16,2048]{0,1:T(8,128)}) %all-reduce.6.cloned.1.call-update) | async-done | bytes 131088 | tf_op jit(solution)/shard_map/psum | solution.py:80
  1068.2 1.3 fusion.27
  1069.5 0.8 copy.33
  1070.3 0.8 copy.34
  (13 shorter events, 0.1 us)
Async XLA Ops:
  8.0 1.6 copy-start
  8.0 964.6 %reduce-scatter.4.cloned.1.call-start = ((), (), s32[]{:S(2)}) async-start(), calls=%async_computation.3 | async-start | bytes 8519680
  285.2 4.0 copy-start.2
  554.1 13.0 %copy-start.4 = (bf16[8,768,128]{1,2,0:T(8,128)(2,1)}, bf16[8,768,128]{1,2,0:T(8,128)(2,1)S(1)}, u32[]{:S(2)}) copy-start(bf16[8,768,128]{1,2,0:T(8,128)(2,1)S(1)} %fusion.12) | copy-start | bytes 4718596
  564.5 2.7 copy-start.1
  564.5 3.8 copy-start.3
  567.1 1.1 copy-start.5
  584.5 396.5 %all-reduce.4.cloned.1.call-start = ((), (), s32[]{:S(2)}) async-start(), calls=%async_computation.1 | async-start | bytes 4194304 | tf_op jit(solution)/shard_map/psum | solution.py:85
  593.2 475.0 %all-reduce.6.cloned.1.call-start = ((), (), s32[]{:S(2)}) async-start(), calls=%async_computation.2 | async-start | bytes 2097152 | tf_op jit(solution)/shard_map/psum | solution.py:80
Sparse Core Ops, SparseCore 0:
  584.6 387.9 reduce-scatter.3
Sparse Core Ops, SparseCore 1:
  593.3 370.9 all-reduce.3
  975.0 93.2 all-reduce.5
where the time goes:
time: 1080 us
  blocking collectives  506 us (47%)
  waiting for transfers between devices  460 us (43%)
  matrix products  58.6 us (5%)
  local copies, waits for them, and re-layouts  28.1 us (3%)
  between operations  15.6 us (1%)
    unnamed x4, waiting for transfers between devices  374 us
    pmax x1, blocking collectives, body(): global_top = lax.pmax(local_top, 'seq')  257 us
    psum x1, blocking collectives, body(): row_total, delta_raw = lax.psum((part_total, part_delta), 'seq')  248 us
    psum x1, waiting for transfers between devices, body(): weight_sums = lax.psum(weight_part, 'batch')  85.9 us
  transfers between devices with their start and end apart: 3, of which 2 were waited for; matrix products, arithmetic and copies ran while one was open for 2% of the time, Pallas kernels for 0%

commit v1 on v0

v1 whole, which is shorter than its diff:
```python
import math

import jax
import jax.numpy as jnp
import numpy as np
from jax import lax
from jax.experimental import pallas as pl
from jax.experimental.pallas import tpu as pltpu
from jax.sharding import PartitionSpec as P

L = 512
D = 1024
HS = 128
HD = 4
W = HD * HS
MP = 768
CH = 256
SCALE = 1.0 / math.sqrt(128.0)
EXP2 = SCALE * math.log2(math.e)
BF = jnp.bfloat16
F32 = jnp.float32
AXES = ("seq", "batch")
NT = (((1,), (1,)), ((), ()))
TN = (((0,), (0,)), ((), ()))


def routes(move):
    pairs = []
    for seq in range(64):
        for batch in range(4):
            yl, x, z = seq // 32, seq // 8 % 4, seq % 8
            yh, c = batch // 2, batch % 2
            y, x, z, c = move(yh * 2 + yl, x, z, c)
            y, x, z, c = y % 4, x % 4, z % 8, c % 2
            pairs.append((seq * 4 + batch, (((y % 2) * 4 + x) * 8 + z) * 4 + (y // 2) * 2 + c))
    return pairs


def send(value, move):
    return lax.ppermute(value, AXES, routes(move))


def attend_kernel(pos, x_ref, wk_ref, wv_ref, q_ref, cot_ref, k_ref, e_ref, g_ref, st_ref, s_buf, p_buf):
    x = x_ref[...].astype(BF)
    k = jnp.dot(x, wk_ref[...], preferred_element_type=F32).astype(BF)
    v = jnp.dot(x, wv_ref[...], preferred_element_type=F32).astype(BF)
    k_ref[...] = k
    tops, totals, deltas = [], [], []
    for j in range(2):
        cols = slice(j * HS, (j + 1) * HS)
        kj, vj, qj, cj = k[:, cols], v[:, cols], q_ref[:, cols], cot_ref[:, cols].astype(BF)
        top = jnp.full((8, L), -jnp.inf, F32)
        for r in range(0, MP, CH):
            s = lax.dot_general(kj[r : r + CH], qj, NT, preferred_element_type=F32)
            s_buf[r : r + CH] = s
            p_buf[r : r + CH] = lax.dot_general(vj[r : r + CH], cj, NT, preferred_element_type=F32)
            top = jnp.maximum(top, jnp.max(s.reshape(CH // 8, 8, L), axis=0))
        top = jnp.max(top, axis=0, keepdims=True)
        total = jnp.zeros((8, L), F32)
        delta = jnp.zeros((8, L), F32)
        step = 64
        for r in range(0, MP, step):
            p = jnp.exp2((s_buf[r : r + step] - top) * EXP2)
            dp = p_buf[r : r + step]
            s_buf[r : r + step] = p
            e_ref[r : r + step, j * L : (j + 1) * L] = p.astype(BF)
            total += jnp.sum(p.reshape(step // 8, 8, L), axis=0)
            delta += jnp.sum((p * dp).reshape(step // 8, 8, L), axis=0)
        total = jnp.sum(total, axis=0, keepdims=True)
        delta = jnp.sum(delta, axis=0, keepdims=True)
        mean = delta / total
        for r in range(0, MP, step):
            g_ref[r : r + step, j * L : (j + 1) * L] = (
                s_buf[r : r + step] * (p_buf[r : r + step] - mean)
            ).astype(BF)
        tops.append(top)
        totals.append(total)
        deltas.append(delta)
    st_ref[0] = jnp.concatenate(tops + totals + deltas + [jnp.zeros((2, L), F32)], axis=0)


def attend(pos, x, wk, wv, q, cot, cot_slot):
    mine = lambda g, pos: (0, pos[0] * 2 + g)
    here = lambda g, pos: (0, g)
    return pl.pallas_call(
        attend_kernel,
        grid_spec=pltpu.PrefetchScalarGridSpec(
            num_scalar_prefetch=1,
            grid=(2,),
            in_specs=[
                pl.BlockSpec((MP, D), lambda g, pos: (0, 0)),
                pl.BlockSpec((D, 2 * HS), mine),
                pl.BlockSpec((D, 2 * HS), mine),
                pl.BlockSpec((L, 2 * HS), mine),
                pl.BlockSpec((L, 2 * HS), mine if cot_slot else here),
            ],
            out_specs=[
                pl.BlockSpec((MP, 2 * HS), here),
                pl.BlockSpec((MP, 2 * L), here),
                pl.BlockSpec((MP, 2 * L), here),
                pl.BlockSpec((1, 8, L), lambda g, pos: (g, 0, 0)),
            ],
            scratch_shapes=[pltpu.VMEM((MP, L), F32), pltpu.VMEM((MP, L), F32)],
        ),
        out_shape=[
            jax.ShapeDtypeStruct((MP, W), BF),
            jax.ShapeDtypeStruct((MP, HD * L), BF),
            jax.ShapeDtypeStruct((MP, HD * L), BF),
            jax.ShapeDtypeStruct((2, 8, L), F32),
        ],
        compiler_params=pltpu.CompilerParams(vmem_limit_bytes=40 * 2**20),
        cost_estimate=pl.CostEstimate(flops=3 * 10**9, bytes_accessed=12 * 10**6, transcendentals=10**6),
    )(pos, x, wk, wv, q, cot)


def latent_kernel(e_ref, g_ref, k_ref, ek_ref, gk_ref):
    k = k_ref[...]
    ek_ref[...] = lax.dot_general(e_ref[...], k, TN, preferred_element_type=F32)
    gk_ref[...] = lax.dot_general(g_ref[...], k, TN, preferred_element_type=F32)


def latent_parts(e, g, k):
    at = lambda j: (0, j)
    return pl.pallas_call(
        latent_kernel,
        grid=(HD,),
        in_specs=[pl.BlockSpec((MP, L), at), pl.BlockSpec((MP, L), at), pl.BlockSpec((MP, HS), at)],
        out_specs=[pl.BlockSpec((L, HS), at), pl.BlockSpec((L, HS), at)],
        out_shape=[jax.ShapeDtypeStruct((L, W), F32)] * 2,
        compiler_params=pltpu.CompilerParams(vmem_limit_bytes=24 * 2**20),
        cost_estimate=pl.CostEstimate(flops=10**9, bytes_accessed=8 * 10**6, transcendentals=0),
    )(e, g, k)


def grads_kernel(
    pos, fac_ref, e0_ref, g0_ref, e1_ref, g1_ref, q_ref, c0_ref, c1_ref, x0_ref, x1_ref,
    ek0_ref, gk0_ref, ek1_ref, gk1_ref,
    r0_ref, r1_ref, r2_ref, r3_ref, d0_ref, d1_ref,
    right, left, wg, lat,
):
    i = pl.program_id(0)
    half = MP // CH

    @pl.when(i == 0)
    def _():
        fac = fac_ref[...].T
        for n, (cot_ref, ek_ref, gk_ref) in enumerate(((c0_ref, ek0_ref, gk0_ref), (c1_ref, ek1_ref, gk1_ref))):
            for j in range(HD):
                cols = slice(j * HS, (j + 1) * HS)
                a = fac[:, n * HD + j : n * HD + j + 1]
                eps = fac[:, 8 + n * HD + j : 8 + n * HD + j + 1]
                aq = a * q_ref[:, cols].astype(F32)
                right[n, j, :, :HS] = (eps * aq).astype(BF)
                right[n, j, :, HS:] = (a * cot_ref[:, cols].astype(F32)).astype(BF)
                left[n, j] = aq.astype(BF)
                part = (a * SCALE) * (gk_ref[:, cols] + eps * ek_ref[:, cols])
                rows, at = (j // 2) * L, (j % 2) * HS
                if n == 0:
                    lat[rows : rows + L, at : at + HS] = part
                else:
                    lat[rows : rows + L, at : at + HS] += part

    def chunk(n, e_ref, g_ref, d_ref, r):
        for j in range(HD):
            cols = slice(j * L, (j + 1) * L)
            both = jnp.dot(e_ref[:, cols], right[n, j], preferred_element_type=F32)
            own = jnp.dot(g_ref[:, cols], left[n, j], preferred_element_type=F32)
            d_ref[pl.ds(r, CH), j * HS : (j + 1) * HS] = ((own + both[:, :HS]) * SCALE).astype(BF)
            d_ref[pl.ds(r, CH), W + j * HS : W + (j + 1) * HS] = both[:, HS:].astype(BF)

    @pl.when(i < half)
    def _():
        chunk(0, e0_ref, g0_ref, d0_ref, pl.multiple_of(i * CH, CH))

    @pl.when(i >= half)
    def _():
        chunk(1, e1_ref, g1_ref, d1_ref, pl.multiple_of((i - half) * CH, CH))

    @pl.when(i == 2 * half - 1)
    def _():
        for r in range(0, D, CH):
            for n in range(0, D, CH):
                wg[r : r + CH, n : n + CH] = jnp.dot(
                    x0_ref[r : r + CH], d0_ref[:, n : n + CH], preferred_element_type=F32
                ) + jnp.dot(x1_ref[r : r + CH], d1_ref[:, n : n + CH], preferred_element_type=F32)
        core, mx, my, mz = pos[0], pos[1], pos[2], pos[3]
        m1 = jnp.where(core == 0, mx, my)
        m2 = jnp.where(core == 0, my, mx)
        for r1, out in enumerate((r0_ref, r1_ref, r2_ref, r3_ref)):
            p1 = lax.rem(m1 + r1, 4)

            def place(t, _, p1=p1, out=out):
                p2 = lax.rem(m2 + t // 8, 4)
                z = lax.rem(mz + t % 8, 8)
                x = jnp.where(core == 0, p1, p2)
                y = jnp.where(core == 0, p2, p1)
                s = (y % 2) * 32 + x * 8 + z
                yh = y // 2
                dst = pl.ds(pl.multiple_of(t * 8, 8), 8)
                out[dst, :D] = wg[pl.ds(pl.multiple_of((s * 2 + yh) * 8, 8), 8), :]
                out[dst, D:] = lat[pl.ds(pl.multiple_of(yh * L + s * 8, 8), 8), :]
                return 0

            lax.fori_loop(0, 32, place, 0)


def grads(pos, fac, e0, g0, e1, g1, q, c0, c1, xt0, xt1, ek0, gk0, ek1, gk1):
    half = MP // CH
    first = lambda i, pos: (jnp.minimum(i, half - 1), 0)
    second = lambda i, pos: (jnp.maximum(i - half, 0), 0)
    fixed = lambda i, pos: (0, 0)
    whole = lambda a: pl.BlockSpec(a.shape, fixed)
    mine = lambda i, pos: (0, pos[0])
    return pl.pallas_call(
        grads_kernel,
        grid_spec=pltpu.PrefetchScalarGridSpec(
            num_scalar_prefetch=1,
            grid=(2 * half,),
            in_specs=[
                whole(fac),
                pl.BlockSpec((CH, HD * L), first),
                pl.BlockSpec((CH, HD * L), first),
                pl.BlockSpec((CH, HD * L), second),
                pl.BlockSpec((CH, HD * L), second),
                pl.BlockSpec((L, W), mine),
                pl.BlockSpec((L, W), mine),
                whole(c1),
                whole(xt0),
                whole(xt1),
                whole(ek0),
                whole(gk0),
                whole(ek1),
                whole(gk1),
            ],
            out_specs=[pl.BlockSpec((256, 1280), fixed)] * 4 + [pl.BlockSpec((MP, D), fixed)] * 2,
            scratch_shapes=[
                pltpu.VMEM((2, HD, L, 2 * HS), BF),
                pltpu.VMEM((2, HD, L, HS), BF),
                pltpu.VMEM((D, D), F32),
                pltpu.VMEM((2 * L, 2 * HS), F32),
            ],
        ),
        out_shape=[jax.ShapeDtypeStruct((256, 1280), F32)] * 4 + [jax.ShapeDtypeStruct((MP, D), BF)] * 2,
        compiler_params=pltpu.CompilerParams(vmem_limit_bytes=56 * 2**20),
        cost_estimate=pl.CostEstimate(flops=6 * 10**9, bytes_accessed=26 * 10**6, transcendentals=0),
    )(pos, fac, e0, g0, e1, g1, q, c0, c1, xt0, xt1, ek0, gk0, ek1, gk1)


def merge(parts):
    top = parts[0][:8]
    for p in parts[1:]:
        top = jnp.maximum(top, p[:8])
    total = delta = 0.0
    for p in parts:
        w = jnp.exp2((p[:8] - top) * EXP2)
        total += w * p[8:16]
        delta += w * p[16:]
    return jnp.concatenate([top, total, delta], axis=0)


def body(queries, inputs, cotangent, key_weight, value_weight):
    seq, batch = lax.axis_index("seq"), lax.axis_index("batch")
    yl, mx, mz = seq // 32, seq // 8 % 4, seq % 8
    yh, core = batch // 2, batch % 2
    pos = jnp.stack([core, mx, yh * 2 + yl, mz]).astype(jnp.int32)
    x0, c0 = inputs[0], cotangent[0]

    over = lambda y, x, z, c: (y, x, z, c + 1)
    x1 = send(x0.astype(F32), over)
    c1 = send(lax.dynamic_slice(c0, (0, (1 - core) * W), (L, W)).astype(F32), over)

    k0, e0, g0, st0 = attend(pos, x0, key_weight, value_weight, queries, c0, True)
    k1, e1, g1, st1 = attend(pos, x1, key_weight, value_weight, queries, c1, False)
    local = jnp.concatenate(
        [s[:, r : r + 2].reshape(4, L) for r in (0, 2, 4) for s in (st0, st1)], axis=0
    )
    stats = local
    stats = merge([stats] + [send(stats, lambda y, x, z, c, n=n: (y, x + n, z, c)) for n in (1, 2, 3)])
    stats = merge([stats] + [send(stats, lambda y, x, z, c, n=n: (y, x, z + n, c)) for n in (2, 4, 6)])
    stats = merge(
        [stats]
        + [send(stats, lambda y, x, z, c, n=n: (y ^ (n & 1), x, z ^ (n >> 1), c)) for n in (1, 2, 3)]
    )

    ek0, gk0 = latent_parts(e0, g0, k0)
    ek1, gk1 = latent_parts(e1, g1, k1)
    xt0, xt1 = x0.T, x1.T.astype(BF)
    own_weight = jnp.concatenate(
        [lax.dynamic_slice(w, (0, core * W), (D, W)) for w in (key_weight, value_weight)], axis=1
    )

    a = jnp.exp2((local[:8] - stats[:8]) * EXP2) / stats[8:16]
    eps = local[16:] / local[8:16] - stats[16:] / stats[8:16]
    fac = jnp.concatenate([a, eps], axis=0)
    r0, r1, r2, r3, d0, d1 = grads(
        pos, fac, e0, g0, e1, g1, queries, c0, c1, xt0, xt1, ek0, gk0, ek1, gk1
    )

    def first(n):
        return lambda y, x, z, c: (y, x + n, z, c) if c == 0 else (y + n, x, z, c)

    def second(n):
        return lambda y, x, z, c: (y + n, x, z, c) if c == 0 else (y, x + n, z, c)

    got = [send(r, first(n)) for n, r in ((2, r2), (1, r1), (3, r3))]
    part = [sum((g[64 * n : 64 * n + 64] for g in got), r0[64 * n : 64 * n + 64]) for n in range(4)]
    got = [send(part[n], second(n)) for n in (2, 1, 3)]
    part = [sum((g[16 * n : 16 * n + 16] for g in got), part[0][16 * n : 16 * n + 16]) for n in range(4)]
    got = [send(part[n], lambda y, x, z, c, n=n: (y, x, z + 2 * n, c)) for n in (2, 1, 3)]
    part = [sum((g[8 * n : 8 * n + 8] for g in got), part[0][8 * n : 8 * n + 8]) for n in range(2)]
    mine = part[0] + send(part[1], lambda y, x, z, c: (y, x, z + 1, c))

    theirs = send(mine, over)
    pair = jnp.where(
        core == 0, jnp.concatenate([mine, theirs], axis=1), jnp.concatenate([theirs, mine], axis=1)
    )
    far = send(pair, lambda y, x, z, c: (y + 2, x, z, c))
    low, high = jnp.where(yh == 0, pair, far), jnp.where(yh == 0, far, pair)
    sums = jnp.concatenate([low, high], axis=0)
    key_grad = jnp.concatenate([sums[:, :512], sums[:, 1280:1792]], axis=1)
    value_grad = jnp.concatenate([sums[:, 512:1024], sums[:, 1792:2304]], axis=1)
    latent_grad = jnp.concatenate(
        [low[:, 1024:1280], high[:, 1024:1280], low[:, 2304:], high[:, 2304:]], axis=1
    )

    away = lax.dot_general(d1, own_weight, NT, preferred_element_type=F32)
    home = lax.dot_general(d0, own_weight, NT, preferred_element_type=F32)
    grad_in = (home + send(away, over)).astype(BF)
    return grad_in[None], latent_grad, key_grad, value_grad


def solution(mesh):
    placed = (P(), P("batch", "seq", None), P("batch", None, None), P(), P())
    return jax.shard_map(
        body,
        mesh=mesh,
        in_specs=placed,
        out_specs=(P("batch", "seq", None), P("seq", None), P("seq", None), P("seq", None)),
        check_vma=False,
    )
```

time: 1080 us -> 186 us (0.17)
  blocking collectives: 506 us -> 0 us
  waiting for transfers between devices: 460 us -> 40.3 us
  matrix products: 58.6 us -> 8.84 us
  Pallas kernels: 0 us -> 47.8 us
  starting transfers between devices: 0.35 us -> 47 us
  between operations: 15.6 us -> 0.97 us
    unnamed x4 -> x0, waiting for transfers between devices: 374 us -> none
    pmax x1 -> x0, blocking collectives: 257 us -> none  [body(): global_top = lax.pmax(local_top, 'seq')]
    psum x1 -> x0, blocking collectives: 248 us -> none  [body(): row_total, delta_raw = lax.psum((part_total, part_delta), 'seq')]
    psum x2 -> x0, waiting for transfers between devices: 85.9 us -> none  [the longest x1 85.9 us: body(): weight_sums = lax.psum(weight_part, 'batch')]
    dot_general x10 -> x2, matrix products: 58.6 us -> 8.84 us  [the longest x1 5.33 us: body(): home = lax.dot_general(d0, own_weight, NT, preferred_element_type=F32)]
    pallas_call x0 -> x5, Pallas kernels: none -> 47.8 us  [the longest x1 24 us: grads(): pl.pallas_call(grads_kernel, grid_spec=pltpu.PrefetchScalarGridSpec(num_s...]
    ppermute x0 -> x24, starting transfers between devices: none -> 47 us  [send(): return lax.ppermute(value, AXES, routes(move))]
    ppermute x0 -> x24, waiting for transfers between devices: none -> 40.3 us  [send(): return lax.ppermute(value, AXES, routes(move))]
  transfers between devices with their start and end apart: 3 -> 24, of which waited for: 2 -> 9; matrix products, arithmetic and copies ran while one was open for 2% -> 8% of each run, Pallas kernels for 0% -> 8%
where the time goes in v1:
time: 186 us
  Pallas kernels  47.8 us (26%)
  starting transfers between devices  47 us (25%)
  waiting for transfers between devices  40.3 us (22%)
  local copies, waits for them, and re-layouts  30 us (16%)
  other arithmetic  10.7 us (6%)
  matrix products  8.84 us (5%)
    ppermute x24, starting transfers between devices, send(): return lax.ppermute(value, AXES, routes(move))  47 us
    ppermute x24, waiting for transfers between devices, send(): return lax.ppermute(value, AXES, routes(move))  40.3 us
    pallas_call x1, Pallas kernels, grads(): pl.pallas_call(grads_kernel, grid_spec=pltpu.PrefetchScalarGridSpec(num_s...  24 us
    unnamed x65, local copies, waits for them, and re-layouts  23.6 us
    pallas_call x2, Pallas kernels, attend(): pl.pallas_call(attend_kernel, grid_spec=pltpu.PrefetchScalarGridSpec(num_...  17.2 us
    pallas_call x2, Pallas kernels, latent_parts(): pl.pallas_call(latent_kernel, grid=(HD,), in_specs=[pl.BlockSpec((MP, L),...  6.69 us
    dot_general x1, matrix products, body(): home = lax.dot_general(d0, own_weight, NT, preferred_element_type=F32)  5.33 us
    ppermute x1, local copies, waits for them, and re-layouts, send(): return lax.ppermute(value, AXES, routes(move))  4.66 us
  transfers between devices with their start and end apart: 24, of which 9 were waited for; matrix products, arithmetic and copies ran while one was open for 8% of the time, Pallas kernels for 8%

profile of v1, /device:TPU:1, one launch (start us, length us, event | category | flops | bytes accessed | tf_op | source)
XLA Modules:
  0.0 185.5 jit_solution(11649566489641823464)
XLA Ops:
  2.4 1.9 %bitcast_convert_fusion = f32[768,1024]{0,1:T(8,128)} fusion(bf16[1,768,1024]{1,2,0:T(8,128)(2,1)S(1)} %copy.9), kind=kLoop, calls=%fused_computation.2 | loop fusion | flops 786432 | bytes 4718592 | tf_op jit(solution)/shard_map/convert_element_type | solution.py:269
  4.5 3.2 %collective-permute-start = (f32[768,1024]{0,1:T(8,128)}, f32[768,1024]{0,1:T(8,128)}, u32[]{:S(2)}, u32[]{:S(2)}) collective-permute-start(f32[768,1024]{0,1:T(8,128)} %bitcast_convert_fusion), channel_id=1, source_target_pairs={{0,1},{1,0},{2,3},{3,2},{4,5},{5,4},{6,7},{7,6},{8,9},{9,8},{10,11... | collective-permute-start | bytes 9437192 | tf_op jit(solution)/shard_map/ppermute | solution.py:40
  16.0 8.2 %shard_map.84 = (bf16[768,512]{1,0:T(8,128)(2,1)S(1)}, bf16[768,2048]{1,0:T(8,128)(2,1)S(1)}, bf16[768,2048]{1,0:T(8,128)(2,1)}, f32[2,8,512]{2,1,0:T(8,128)S(1)}) custom-call(s32[4]{0:T(128)S(1)} %pad_add_fusion.pos, bf16[768,1024]{1,0:T(8,128)(2,1)S(1)} %bitcast.21, bf16[1024,1024]{1,0:T(8,128)(2,1)S(1)} %copy-done.19, bf16[1024,1024]{1,0:T(8,128)(2,1)S(1)} %copy-done.22, ...), custom_call_target="tpu_custom_call" | custom-call | flops 3000000000 | bytes 12000000 | tf_op jit(solution)/shard_map/pallas_call | solution.py:85
  25.2 4.7 %copy.11.x_ref = f32[768,1024]{1,0:T(8,128)} copy(f32[768,1024]{0,1:T(8,128)} %collective-permute-done) | data formatting | bytes 6291456 | tf_op jit(solution)/shard_map/ppermute | solution.py:40
  34.2 9.0 %shard_map.85 = (bf16[768,512]{1,0:T(8,128)(2,1)S(1)}, bf16[768,2048]{1,0:T(8,128)(2,1)S(1)}, bf16[768,2048]{1,0:T(8,128)(2,1)S(1)}, f32[2,8,512]{2,1,0:T(8,128)S(1)}) custom-call(s32[4]{0:T(128)S(1)} %pad_add_fusion.pos, f32[768,1024]{1,0:T(8,128)} %copy.11.x_ref, bf16[1024,1024]{1,0:T(8,128)(2,1)S(1)} %copy-done.20, bf16[1024,1024]{1,0:T(8,128)(2,1)S(1)} %copy-done.23, ...), custom_call_target="tpu_custom_call" | custom-call | flops 3000000000 | bytes 12000000 | tf_op jit(solution)/shard_map/pallas_call | solution.py:85
  47.8 1.9 %collective-permute-start.3 = (f32[24,512]{1,0:T(8,128)S(1)}, f32[24,512]{1,0:T(8,128)S(1)}, u32[]{:S(2)}, u32[]{:S(2)}) collective-permute-start(f32[24,512]{1,0:T(8,128)S(1)} %concatenate.43), channel_id=1, source_target_pairs={{0,64},{1,65},{2,66},{3,67},{4,68},{5,69},{6,70},{7,71},{8,72},{9,... | collective-permute-start | bytes 147464 | tf_op jit(solution)/shard_map/ppermute | solution.py:40
  50.8 1.9 %copy-done.1 = bf16[768,2048]{1,0:T(8,128)(2,1)S(1)} copy-done((bf16[768,2048]{1,0:T(8,128)(2,1)S(1)}, bf16[768,2048]{1,0:T(8,128)(2,1)}, u32[]{:S(2)}) %copy-start.1) | copy-done | bytes 3145752
  53.9 3.3 %shard_map.86 = (f32[512,512]{1,0:T(8,128)S(1)}, f32[512,512]{1,0:T(8,128)S(1)}) custom-call(bf16[768,2048]{1,0:T(8,128)(2,1)S(1)} %get-tuple-element.24.e_ref.e0_ref, bf16[768,2048]{1,0:T(8,128)(2,1)S(1)} %copy-done.1, bf16[768,512]{1,0:T(8,128)(2,1)S(1)} %copy-done.18), custom_call_target="tpu_custom_call" | custom-call | flops 1000000000 | bytes 8000000 | tf_op jit(solution)/shard_map/pallas_call | solution.py:124
  57.4 3.3 %collective-permute-start.5 = (f32[24,512]{1,0:T(8,128)S(1)}, f32[24,512]{1,0:T(8,128)S(1)}, u32[]{:S(2)}, u32[]{:S(2)}) collective-permute-start(f32[24,512]{1,0:T(8,128)S(1)} %pad_maximum_fusion.3), channel_id=1, source_target_pairs={{0,8},{1,9},{2,10},{3,11},{4,12},{5,13},{6,14},{7,15},{8,16},{9,17... | collective-permute-start | bytes 147464 | tf_op jit(solution)/shard_map/ppermute | solution.py:40
  60.6 5.1 %collective-permute-start.6 = (f32[24,512]{1,0:T(8,128)S(1)}, f32[24,512]{1,0:T(8,128)S(1)}, u32[]{:S(2)}, u32[]{:S(2)}) collective-permute-start(f32[24,512]{1,0:T(8,128)S(1)} %pad_maximum_fusion.3), channel_id=1, source_target_pairs={{0,16},{1,17},{2,18},{3,19},{4,20},{5,21},{6,22},{7,23},{8,24},{9,... | collective-permute-start | bytes 147464 | tf_op jit(solution)/shard_map/ppermute | solution.py:40
  65.7 2.4 %collective-permute-start.7 = (f32[24,512]{1,0:T(8,128)S(1)}, f32[24,512]{1,0:T(8,128)S(1)}, u32[]{:S(2)}, u32[]{:S(2)}) collective-permute-start(f32[24,512]{1,0:T(8,128)S(1)} %pad_maximum_fusion.3), channel_id=1, source_target_pairs={{0,24},{1,25},{2,26},{3,27},{4,28},{5,29},{6,30},{7,31},{8,0},{9,1... | collective-permute-start | bytes 147464 | tf_op jit(solution)/shard_map/ppermute | solution.py:40
  68.1 3.2 %convert_bitcast_fusion.x1_ref = bf16[1024,768]{1,0:T(8,128)(2,1)} fusion(f32[768,1024]{0,1:T(8,128)} %collective-permute-done), kind=kLoop, calls=%fused_computation.3 | loop fusion | flops 786432 | bytes 4718592 | tf_op jit(solution)/shard_map/convert_element_type | solution.py:287
  71.4 1.8 collective-permute-start.10
  74.2 3.3 %shard_map.87 = (f32[512,512]{1,0:T(8,128)S(1)}, f32[512,512]{1,0:T(8,128)S(1)}) custom-call(bf16[768,2048]{1,0:T(8,128)(2,1)S(1)} %copy-done.3, bf16[768,2048]{1,0:T(8,128)(2,1)S(1)} %copy-done.5, bf16[768,512]{1,0:T(8,128)(2,1)S(1)} %copy-done.16), custom_call_target="tpu_custom_call" | custom-call | flops 1000000000 | bytes 8000000 | tf_op jit(solution)/shard_map/pallas_call | solution.py:124
  80.2 24.0 %shard_map.88 = (f32[256,1280]{1,0:T(8,128)}, f32[256,1280]{1,0:T(8,128)}, f32[256,1280]{1,0:T(8,128)}, f32[256,1280]{1,0:T(8,128)}, bf16[768,1024]{1,0:T(8,128)(2,1)}, /*index=5*/bf16[768,1024]{1,0:T(8,128)(2,1)}) custom-call(s32[4]{0:T(128)} %copy-done.24, f32[16,512]{1,0:T(8,128)} %pad_maximum_fusion.5.fac_ref, bf16[768,2048]{1,0:T(8,128)(2,1)} %copy-done, ...), custom_call_target="tpu_custom_call" | custom-call | flops 6000000000 | bytes 26000000 | tf_op jit(solution)/shard_map/pallas_call | solution.py:214
  104.2 3.0 %collective-permute-start.12 = (f32[256,1280]{1,0:T(8,128)}, f32[256,1280]{1,0:T(8,128)S(1)}, u32[]{:S(2)}, u32[]{:S(2)}) collective-permute-start(f32[256,1280]{1,0:T(8,128)} %get-tuple-element.37), channel_id=1, source_target_pairs={{0,64},{1,3},{2,66},{3,1},{4,68},{5,7},{6,70},{7,5},{8,72},{9,11},... | collective-permute-start | bytes 3932168 | tf_op jit(solution)/shard_map/ppermute | solution.py:40
  107.6 2.3 %collective-permute-start.14 = (f32[256,1280]{1,0:T(8,128)}, f32[256,1280]{1,0:T(8,128)}, u32[]{:S(2)}, u32[]{:S(2)}) collective-permute-start(f32[256,1280]{1,0:T(8,128)} %get-tuple-element.39), channel_id=1, source_target_pairs={{0,96},{1,131},{2,98},{3,129},{4,100},{5,135},{6,102},{7,133},{8,1... | collective-permute-start | bytes 3932168 | tf_op jit(solution)/shard_map/ppermute | solution.py:40
  111.4 11.4 %collective-permute-done.12 = f32[256,1280]{1,0:T(8,128)S(1)} collective-permute-done((f32[256,1280]{1,0:T(8,128)}, f32[256,1280]{1,0:T(8,128)S(1)}, u32[]{:S(2)}, u32[]{:S(2)}) %collective-permute-start.12) | collective-permute-done | bytes 1310752 | tf_op jit(solution)/shard_map/ppermute | solution.py:40
  122.8 14.1 %collective-permute-done.13 = f32[256,1280]{1,0:T(8,128)} collective-permute-done((f32[256,1280]{1,0:T(8,128)}, f32[256,1280]{1,0:T(8,128)}, u32[]{:S(2)}, u32[]{:S(2)}) %collective-permute-start.13) | collective-permute-done | bytes 1310752 | tf_op jit(solution)/shard_map/ppermute | solution.py:40
  137.3 2.1 %slice_add_fusion.9 = (f32[64,1280]{1,0:T(8,128)S(1)}, f32[64,1280]{1,0:T(8,128)S(1)}, f32[64,1280]{1,0:T(8,128)S(1)}, f32[64,1280]{1,0:T(8,128)S(1)}) fusion(f32[256,1280]{1,0:T(8,128)} %collective-permute-done.14, f32[256,1280]{1,0:T(8,128)} %collective-permute-done.13, f32[256,1280]{1,0:T(8,128)S(1)} %collective-permute-done.12, f32[256,1280]{1,0:T(8,128)S(1)} %copy-done.26), kind=kLoop, calls=%fused_computation.16 | loop fusion | flops 983040 | bytes 6553600 | tf_op jit(solution)/shard_map/add | solution.py:306
  140.0 2.3 %collective-permute-start.17 = (f32[64,1280]{1,0:T(8,128)S(1)}, f32[64,1280]{1,0:T(8,128)S(1)}, u32[]{:S(2)}, u32[]{:S(2)}) collective-permute-start(f32[64,1280]{1,0:T(8,128)S(1)} %get-tuple-element.45), channel_id=1, source_target_pairs={{0,130},{1,97},{2,128},{3,99},{4,134},{5,101},{6,132},{7,103},{8,1... | collective-permute-start | bytes 983048 | tf_op jit(solution)/shard_map/ppermute | solution.py:40
  142.4 3.5 %fusion.1 = f32[768,1024]{1,0:T(8,128)} fusion(bf16[768,1024]{1,0:T(8,128)(2,1)S(1)} %copy-done.31, bf16[1024,512]{1,0:T(8,128)(2,1)S(1)} %get-tuple-element.66, bf16[1024,512]{1,0:T(8,128)(2,1)S(1)} %get-tuple-element.67), kind=kOutput, calls=%fused_computation.5 | convolution fusion | flops 1614807040 | bytes 6815744 | tf_op jit(solution)/shard_map/dot_general | solution.py:326
  145.9 7.0 %collective-permute-start.11 = (f32[768,1024]{1,0:T(8,128)}, f32[768,1024]{1,0:T(8,128)}, u32[]{:S(2)}, u32[]{:S(2)}) collective-permute-start(f32[768,1024]{1,0:T(8,128)} %fusion.1), channel_id=1, source_target_pairs={{0,1},{1,0},{2,3},{3,2},{4,5},{5,4},{6,7},{7,6},{8,9},{9,8},{10,11... | collective-permute-start | bytes 9437192 | tf_op jit(solution)/shard_map/ppermute | solution.py:40
  153.0 2.5 %collective-permute-start.18 = (f32[16,1280]{1,0:T(8,128)S(1)}, f32[16,1280]{1,0:T(8,128)S(1)}, u32[]{:S(2)}, u32[]{:S(2)}) collective-permute-start(f32[16,1280]{1,0:T(8,128)S(1)} %get-tuple-element.51), channel_id=1, source_target_pairs={{0,16},{1,17},{2,18},{3,19},{4,20},{5,21},{6,22},{7,23},{8,24},{9,... | collective-permute-start | bytes 245768 | tf_op jit(solution)/shard_map/ppermute | solution.py:40
  155.5 2.9 %collective-permute-start.19 = (f32[16,1280]{1,0:T(8,128)S(1)}, f32[16,1280]{1,0:T(8,128)S(1)}, u32[]{:S(2)}, u32[]{:S(2)}) collective-permute-start(f32[16,1280]{1,0:T(8,128)S(1)} %get-tuple-element.50), channel_id=1, source_target_pairs={{0,8},{1,9},{2,10},{3,11},{4,12},{5,13},{6,14},{7,15},{8,16},{9,17... | collective-permute-start | bytes 245768 | tf_op jit(solution)/shard_map/ppermute | solution.py:40
  160.4 2.7 %collective-permute-done.19 = f32[16,1280]{1,0:T(8,128)S(1)} collective-permute-done((f32[16,1280]{1,0:T(8,128)S(1)}, f32[16,1280]{1,0:T(8,128)S(1)}, u32[]{:S(2)}, u32[]{:S(2)}) %collective-permute-start.19) | collective-permute-done | bytes 81952 | tf_op jit(solution)/shard_map/ppermute | solution.py:40
  163.1 2.3 %collective-permute-done.20 = f32[16,1280]{1,0:T(8,128)S(1)} collective-permute-done((f32[16,1280]{1,0:T(8,128)S(1)}, f32[16,1280]{1,0:T(8,128)S(1)}, u32[]{:S(2)}, u32[]{:S(2)}) %collective-permute-start.20) | collective-permute-done | bytes 81952 | tf_op jit(solution)/shard_map/ppermute | solution.py:40
  165.5 4.0 %collective-permute-done.21 = f32[8,1280]{1,0:T(8,128)S(1)} collective-permute-done((f32[8,1280]{1,0:T(8,128)S(1)}, f32[8,1280]{1,0:T(8,128)S(1)}, u32[]{:S(2)}, u32[]{:S(2)}) %collective-permute-start.21) | collective-permute-done | bytes 40992 | tf_op jit(solution)/shard_map/ppermute | solution.py:40
  169.6 3.2 %collective-permute-start.22 = (f32[8,1280]{1,0:T(8,128)S(1)}, f32[8,1280]{1,0:T(8,128)S(1)}, u32[]{:S(2)}, u32[]{:S(2)}) collective-permute-start(f32[8,1280]{1,0:T(8,128)S(1)} %fusion.4), channel_id=1, source_target_pairs={{0,1},{1,0},{2,3},{3,2},{4,5},{5,4},{6,7},{7,6},{8,9},{9,8},{10,11... | collective-permute-start | bytes 122888 | tf_op jit(solution)/shard_map/ppermute | solution.py:40
  173.6 2.1 %collective-permute-start.23 = (f32[8,2560]{1,0:T(8,128)S(1)}, f32[8,2560]{1,0:T(8,128)S(1)}, u32[]{:S(2)}, u32[]{:S(2)}) collective-permute-start(f32[8,2560]{1,0:T(8,128)S(1)} %maximum_select_fusion), channel_id=1, source_target_pairs={{0,2},{1,3},{2,0},{3,1},{4,6},{5,7},{6,4},{7,5},{8,10},{9,11},{10,... | collective-permute-start | bytes 245768 | tf_op jit(solution)/shard_map/ppermute | solution.py:40
  175.7 3.2 %collective-permute-done.23 = f32[8,2560]{1,0:T(8,128)S(1)} collective-permute-done((f32[8,2560]{1,0:T(8,128)S(1)}, f32[8,2560]{1,0:T(8,128)S(1)}, u32[]{:S(2)}, u32[]{:S(2)}) %collective-permute-start.23) | collective-permute-done | bytes 81952 | tf_op jit(solution)/shard_map/ppermute | solution.py:40
  180.2 5.3 %fusion = bf16[1,768,1024]{2,1,0:T(8,128)(2,1)} fusion(f32[768,1024]{1,0:T(8,128)} %collective-permute-done.11, bf16[768,1024]{1,0:T(8,128)(2,1)} %get-tuple-element.34, bf16[1024,512]{1,0:T(8,128)(2,1)S(1)} %copy-done.28, bf16[1024,512]{1,0:T(8,128)(2,1)S(1)} %copy-done.30), kind=kOutput, calls=%fused_computation.4 | convolution fusion | flops 1616379904 | bytes 8388608 | tf_op jit(solution)/shard_map/dot_general | solution.py:327
  (121 shorter events, 33.5 us)
Async XLA Ops:
  4.5 20.6 %collective-permute-start = (f32[768,1024]{0,1:T(8,128)}, f32[768,1024]{0,1:T(8,128)}, u32[]{:S(2)}, u32[]{:S(2)}) collective-permute-start(f32[768,1024]{0,1:T(8,128)} %bitcast_convert_fusion), channel_id=1, source_target_pairs={{0,1},{1,0},{2,3},{3,2},{4,5},{5,4},{6,7},{7,6},{8,9},{9,8},{10,11... | collective-permute-start | bytes 9437192 | tf_op jit(solution)/shard_map/ppermute | solution.py:40
  8.9 21.0 %collective-permute-start.1 = (f32[512,512]{1,0:T(8,128)}, f32[512,512]{1,0:T(8,128)}, u32[]{:S(2)}, u32[]{:S(2)}) collective-permute-start(f32[512,512]{1,0:T(8,128)} %bitcast_convert_fusion.1), channel_id=1, source_target_pairs={{0,1},{1,0},{2,3},{3,2},{4,5},{5,4},{6,7},{7,6},{8,9},{9,8},{10,11... | collective-permute-start | bytes 3145736 | tf_op jit(solution)/shard_map/ppermute | solution.py:40
  8.9 20.9 %copy-start.24 = (s32[4]{0:T(128)}, s32[4]{0:T(128)S(1)}, u32[]{:S(2)}) copy-start(s32[4]{0:T(128)S(1)} %pad_add_fusion.pos) | copy-start | bytes 52
  25.1 25.7 %copy-start = (bf16[768,2048]{1,0:T(8,128)(2,1)}, bf16[768,2048]{1,0:T(8,128)(2,1)S(1)}, u32[]{:S(2)}) copy-start(bf16[768,2048]{1,0:T(8,128)(2,1)S(1)} %get-tuple-element.24.e_ref.e0_ref) | copy-start | bytes 9437188
  47.7 9.6 %collective-permute-start.2 = (f32[24,512]{1,0:T(8,128)S(1)}, f32[24,512]{1,0:T(8,128)S(1)}, u32[]{:S(2)}, u32[]{:S(2)}) collective-permute-start(f32[24,512]{1,0:T(8,128)S(1)} %concatenate.43), channel_id=1, source_target_pairs={{0,32},{1,33},{2,34},{3,35},{4,36},{5,37},{6,38},{7,39},{8,40},{9,... | collective-permute-start | bytes 147464 | tf_op jit(solution)/shard_map/ppermute | solution.py:40
  47.8 9.5 %collective-permute-start.3 = (f32[24,512]{1,0:T(8,128)S(1)}, f32[24,512]{1,0:T(8,128)S(1)}, u32[]{:S(2)}, u32[]{:S(2)}) collective-permute-start(f32[24,512]{1,0:T(8,128)S(1)} %concatenate.43), channel_id=1, source_target_pairs={{0,64},{1,65},{2,66},{3,67},{4,68},{5,69},{6,70},{7,71},{8,72},{9,... | collective-permute-start | bytes 147464 | tf_op jit(solution)/shard_map/ppermute | solution.py:40
  49.7 7.6 %collective-permute-start.4 = (f32[24,512]{1,0:T(8,128)S(1)}, f32[24,512]{1,0:T(8,128)S(1)}, u32[]{:S(2)}, u32[]{:S(2)}) collective-permute-start(f32[24,512]{1,0:T(8,128)S(1)} %concatenate.43), channel_id=1, source_target_pairs={{0,96},{1,97},{2,98},{3,99},{4,100},{5,101},{6,102},{7,103},{8,104... | collective-permute-start | bytes 147464 | tf_op jit(solution)/shard_map/ppermute | solution.py:40
  57.4 14.0 %collective-permute-start.5 = (f32[24,512]{1,0:T(8,128)S(1)}, f32[24,512]{1,0:T(8,128)S(1)}, u32[]{:S(2)}, u32[]{:S(2)}) collective-permute-start(f32[24,512]{1,0:T(8,128)S(1)} %pad_maximum_fusion.3), channel_id=1, source_target_pairs={{0,8},{1,9},{2,10},{3,11},{4,12},{5,13},{6,14},{7,15},{8,16},{9,17... | collective-permute-start | bytes 147464 | tf_op jit(solution)/shard_map/ppermute | solution.py:40
  60.6 10.7 %collective-permute-start.6 = (f32[24,512]{1,0:T(8,128)S(1)}, f32[24,512]{1,0:T(8,128)S(1)}, u32[]{:S(2)}, u32[]{:S(2)}) collective-permute-start(f32[24,512]{1,0:T(8,128)S(1)} %pad_maximum_fusion.3), channel_id=1, source_target_pairs={{0,16},{1,17},{2,18},{3,19},{4,20},{5,21},{6,22},{7,23},{8,24},{9,... | collective-permute-start | bytes 147464 | tf_op jit(solution)/shard_map/ppermute | solution.py:40
  65.7 5.6 %collective-permute-start.7 = (f32[24,512]{1,0:T(8,128)S(1)}, f32[24,512]{1,0:T(8,128)S(1)}, u32[]{:S(2)}, u32[]{:S(2)}) collective-permute-start(f32[24,512]{1,0:T(8,128)S(1)} %pad_maximum_fusion.3), channel_id=1, source_target_pairs={{0,24},{1,25},{2,26},{3,27},{4,28},{5,29},{6,30},{7,31},{8,0},{9,1... | collective-permute-start | bytes 147464 | tf_op jit(solution)/shard_map/ppermute | solution.py:40
  71.4 8.1 %collective-permute-start.10 = (f32[24,512]{1,0:T(8,128)S(1)}, f32[24,512]{1,0:T(8,128)S(1)}, u32[]{:S(2)}, u32[]{:S(2)}) collective-permute-start(f32[24,512]{1,0:T(8,128)S(1)} %pad_maximum_fusion.4), channel_id=1, source_target_pairs={{0,132},{1,133},{2,134},{3,135},{4,128},{5,129},{6,130},{7,131},{8... | collective-permute-start | bytes 147464 | tf_op jit(solution)/shard_map/ppermute | solution.py:40
  73.3 6.2 %collective-permute-start.8 = (f32[24,512]{1,0:T(8,128)S(1)}, f32[24,512]{1,0:T(8,128)S(1)}, u32[]{:S(2)}, u32[]{:S(2)}) collective-permute-start(f32[24,512]{1,0:T(8,128)S(1)} %pad_maximum_fusion.4), channel_id=1, source_target_pairs={{0,128},{1,129},{2,130},{3,131},{4,132},{5,133},{6,134},{7,135},{8... | collective-permute-start | bytes 147464 | tf_op jit(solution)/shard_map/ppermute | solution.py:40
  73.4 6.1 %collective-permute-start.9 = (f32[24,512]{1,0:T(8,128)S(1)}, f32[24,512]{1,0:T(8,128)S(1)}, u32[]{:S(2)}, u32[]{:S(2)}) collective-permute-start(f32[24,512]{1,0:T(8,128)S(1)} %pad_maximum_fusion.4), channel_id=1, source_target_pairs={{0,4},{1,5},{2,6},{3,7},{4,0},{5,1},{6,2},{7,3},{8,12},{9,13},{10,... | collective-permute-start | bytes 147464 | tf_op jit(solution)/shard_map/ppermute | solution.py:40
  80.2 29.6 %copy-start.21 = (bf16[1024,1024]{1,0:T(8,128)(2,1)S(1)}, bf16[1024,1024]{1,0:T(8,128)(2,1)}, u32[]{:S(2)}) copy-start(bf16[1024,1024]{1,0:T(8,128)(2,1)} %wk_ref.3) | copy-start | bytes 6291460
  104.2 18.6 %collective-permute-start.12 = (f32[256,1280]{1,0:T(8,128)}, f32[256,1280]{1,0:T(8,128)S(1)}, u32[]{:S(2)}, u32[]{:S(2)}) collective-permute-start(f32[256,1280]{1,0:T(8,128)} %get-tuple-element.37), channel_id=1, source_target_pairs={{0,64},{1,3},{2,66},{3,1},{4,68},{5,7},{6,70},{7,5},{8,72},{9,11},... | collective-permute-start | bytes 3932168 | tf_op jit(solution)/shard_map/ppermute | solution.py:40
  107.2 29.7 %collective-permute-start.13 = (f32[256,1280]{1,0:T(8,128)}, f32[256,1280]{1,0:T(8,128)}, u32[]{:S(2)}, u32[]{:S(2)}) collective-permute-start(f32[256,1280]{1,0:T(8,128)} %get-tuple-element.38), channel_id=1, source_target_pairs={{0,32},{1,129},{2,34},{3,131},{4,36},{5,133},{6,38},{7,135},{8,40}... | collective-permute-start | bytes 3932168 | tf_op jit(solution)/shard_map/ppermute | solution.py:40
  107.6 29.7 %collective-permute-start.14 = (f32[256,1280]{1,0:T(8,128)}, f32[256,1280]{1,0:T(8,128)}, u32[]{:S(2)}, u32[]{:S(2)}) collective-permute-start(f32[256,1280]{1,0:T(8,128)} %get-tuple-element.39), channel_id=1, source_target_pairs={{0,96},{1,131},{2,98},{3,129},{4,100},{5,135},{6,102},{7,133},{8,1... | collective-permute-start | bytes 3932168 | tf_op jit(solution)/shard_map/ppermute | solution.py:40
  109.8 27.4 %copy-start.26 = (f32[256,1280]{1,0:T(8,128)S(1)}, f32[256,1280]{1,0:T(8,128)}, u32[]{:S(2)}) copy-start(f32[256,1280]{1,0:T(8,128)} %get-tuple-element.36) | copy-start | bytes 3932164
  111.4 31.0 %copy-start.27 = (bf16[1024,512]{1,0:T(8,128)(2,1)}, bf16[1024,512]{1,0:T(8,128)(2,1)S(1)}, u32[]{:S(2)}) copy-start(bf16[1024,512]{1,0:T(8,128)(2,1)S(1)} %get-tuple-element.66) | copy-start | bytes 3145732
  111.4 31.0 %copy-start.29 = (bf16[1024,512]{1,0:T(8,128)(2,1)}, bf16[1024,512]{1,0:T(8,128)(2,1)S(1)}, u32[]{:S(2)}) copy-start(bf16[1024,512]{1,0:T(8,128)(2,1)S(1)} %get-tuple-element.67) | copy-start | bytes 3145732
  139.4 13.5 %collective-permute-start.15 = (f32[64,1280]{1,0:T(8,128)S(1)}, f32[64,1280]{1,0:T(8,128)S(1)}, u32[]{:S(2)}, u32[]{:S(2)}) collective-permute-start(f32[64,1280]{1,0:T(8,128)S(1)} %get-tuple-element.47), channel_id=1, source_target_pairs={{0,2},{1,65},{2,0},{3,67},{4,6},{5,69},{6,4},{7,71},{8,10},{9,73},... | collective-permute-start | bytes 983048 | tf_op jit(solution)/shard_map/ppermute | solution.py:40
  139.7 13.2 %collective-permute-start.16 = (f32[64,1280]{1,0:T(8,128)S(1)}, f32[64,1280]{1,0:T(8,128)S(1)}, u32[]{:S(2)}, u32[]{:S(2)}) collective-permute-start(f32[64,1280]{1,0:T(8,128)S(1)} %get-tuple-element.46), channel_id=1, source_target_pairs={{0,128},{1,33},{2,130},{3,35},{4,132},{5,37},{6,134},{7,39},{8,136... | collective-permute-start | bytes 983048 | tf_op jit(solution)/shard_map/ppermute | solution.py:40
  140.0 12.9 %collective-permute-start.17 = (f32[64,1280]{1,0:T(8,128)S(1)}, f32[64,1280]{1,0:T(8,128)S(1)}, u32[]{:S(2)}, u32[]{:S(2)}) collective-permute-start(f32[64,1280]{1,0:T(8,128)S(1)} %get-tuple-element.45), channel_id=1, source_target_pairs={{0,130},{1,97},{2,128},{3,99},{4,134},{5,101},{6,132},{7,103},{8,1... | collective-permute-start | bytes 983048 | tf_op jit(solution)/shard_map/ppermute | solution.py:40
  145.9 34.3 %copy-start.28 = (bf16[1024,512]{1,0:T(8,128)(2,1)S(1)}, bf16[1024,512]{1,0:T(8,128)(2,1)}, u32[]{:S(2)}) copy-start(bf16[1024,512]{1,0:T(8,128)(2,1)} %copy-done.27) | copy-start | bytes 3145732
  145.9 34.3 %copy-start.30 = (bf16[1024,512]{1,0:T(8,128)(2,1)S(1)}, bf16[1024,512]{1,0:T(8,128)(2,1)}, u32[]{:S(2)}) copy-start(bf16[1024,512]{1,0:T(8,128)(2,1)} %copy-done.29) | copy-start | bytes 3145732
  145.9 34.3 %collective-permute-start.11 = (f32[768,1024]{1,0:T(8,128)}, f32[768,1024]{1,0:T(8,128)}, u32[]{:S(2)}, u32[]{:S(2)}) collective-permute-start(f32[768,1024]{1,0:T(8,128)} %fusion.1), channel_id=1, source_target_pairs={{0,1},{1,0},{2,3},{3,2},{4,5},{5,4},{6,7},{7,6},{8,9},{9,8},{10,11... | collective-permute-start | bytes 9437192 | tf_op jit(solution)/shard_map/ppermute | solution.py:40
  153.0 7.4 %collective-permute-start.18 = (f32[16,1280]{1,0:T(8,128)S(1)}, f32[16,1280]{1,0:T(8,128)S(1)}, u32[]{:S(2)}, u32[]{:S(2)}) collective-permute-start(f32[16,1280]{1,0:T(8,128)S(1)} %get-tuple-element.51), channel_id=1, source_target_pairs={{0,16},{1,17},{2,18},{3,19},{4,20},{5,21},{6,22},{7,23},{8,24},{9,... | collective-permute-start | bytes 245768 | tf_op jit(solution)/shard_map/ppermute | solution.py:40
  155.5 7.6 %collective-permute-start.19 = (f32[16,1280]{1,0:T(8,128)S(1)}, f32[16,1280]{1,0:T(8,128)S(1)}, u32[]{:S(2)}, u32[]{:S(2)}) collective-permute-start(f32[16,1280]{1,0:T(8,128)S(1)} %get-tuple-element.50), channel_id=1, source_target_pairs={{0,8},{1,9},{2,10},{3,11},{4,12},{5,13},{6,14},{7,15},{8,16},{9,17... | collective-permute-start | bytes 245768 | tf_op jit(solution)/shard_map/ppermute | solution.py:40
  158.4 7.0 %collective-permute-start.20 = (f32[16,1280]{1,0:T(8,128)S(1)}, f32[16,1280]{1,0:T(8,128)S(1)}, u32[]{:S(2)}, u32[]{:S(2)}) collective-permute-start(f32[16,1280]{1,0:T(8,128)S(1)} %get-tuple-element.49), channel_id=1, source_target_pairs={{0,24},{1,25},{2,26},{3,27},{4,28},{5,29},{6,30},{7,31},{8,0},{9,1... | collective-permute-start | bytes 245768 | tf_op jit(solution)/shard_map/ppermute | solution.py:40
  165.4 4.1 %collective-permute-start.21 = (f32[8,1280]{1,0:T(8,128)S(1)}, f32[8,1280]{1,0:T(8,128)S(1)}, u32[]{:S(2)}, u32[]{:S(2)}) collective-permute-start(f32[8,1280]{1,0:T(8,128)S(1)} %slice_add_fusion.24), channel_id=1, source_target_pairs={{0,4},{1,5},{2,6},{3,7},{4,8},{5,9},{6,10},{7,11},{8,12},{9,13},{1... | collective-permute-start | bytes 122888 | tf_op jit(solution)/shard_map/ppermute | solution.py:40
  169.6 4.0 %collective-permute-start.22 = (f32[8,1280]{1,0:T(8,128)S(1)}, f32[8,1280]{1,0:T(8,128)S(1)}, u32[]{:S(2)}, u32[]{:S(2)}) collective-permute-start(f32[8,1280]{1,0:T(8,128)S(1)} %fusion.4), channel_id=1, source_target_pairs={{0,1},{1,0},{2,3},{3,2},{4,5},{5,4},{6,7},{7,6},{8,9},{9,8},{10,11... | collective-permute-start | bytes 122888 | tf_op jit(solution)/shard_map/ppermute | solution.py:40
  173.6 5.3 %collective-permute-start.23 = (f32[8,2560]{1,0:T(8,128)S(1)}, f32[8,2560]{1,0:T(8,128)S(1)}, u32[]{:S(2)}, u32[]{:S(2)}) collective-permute-start(f32[8,2560]{1,0:T(8,128)S(1)} %maximum_select_fusion), channel_id=1, source_target_pairs={{0,2},{1,3},{2,0},{3,1},{4,6},{5,7},{6,4},{7,5},{8,10},{9,11},{10,... | collective-permute-start | bytes 245768 | tf_op jit(solution)/shard_map/ppermute | solution.py:40
  (24 other events, 116.5 us)
